TPU v7x, 512 devices: a whole 4x8x8 slice. The times are simulated.
512 devices in a mesh: gx: 8 (over y), gy: 8 (over z_hi, core), gz: 8 (over z_lo, x).
Axes of the slice: x: 4, y: 8, z: 8 (z_hi: 4, z_lo: 2; z = z_hi * 2 + z_lo), core: 2. Of those that a mesh axis runs over, the one named last changes fastest.
Arguments:
- stash: bfloat16 [640, 6144], P(('gy', 'gz'), 'gx'), may hold values from -16 to 16
- mlp_grad: bfloat16 [640, 6144], P(('gy', 'gz'), 'gx'), may hold values from -16 to 16
- qkv_grad: bfloat16 [640, 18432], P('gx', ('gy', 'gz')), may hold values from -16 to 16
- w_gate: bfloat16 [6144, 16384], P('gx', ('gy', 'gz')), may hold values from -0.078125 to 0.078125
- w_up: bfloat16 [6144, 16384], P('gx', ('gy', 'gz')), may hold values from -0.078125 to 0.078125
- w_down: bfloat16 [16384, 6144], P(('gy', 'gz'), 'gx'), may hold values from -0.046875 to 0.046875
- w_qkv: bfloat16 [6144, 18432], P('gx', ('gy', 'gz')), may hold values from -0.078125 to 0.078125
Outputs:
- grad_input: bfloat16 [640, 6144], P(('gy', 'gz'), 'gx')
- grad_gate: bfloat16 [6144, 16384], P('gx', ('gy', 'gz'))
- grad_up: bfloat16 [6144, 16384], P('gx', ('gy', 'gz'))
- grad_down: bfloat16 [16384, 6144], P(('gy', 'gz'), 'gx')
- grad_qkv: bfloat16 [6144, 18432], P('gx', ('gy', 'gz'))
All inputs are finite; a program needn't handle non-finite values.
Results may differ from a plain program's by a relative error of at most 0.0049.
Values may be sent and summed in bfloat16 or wider, within the bound.
A program may use at most 64 MiB of HBM per device.

v0:
```python
import jax
import jax.numpy as jnp
from jax import lax
from jax.sharding import PartitionSpec as P


def contract_rows(left, right):
    return lax.dot_general(
        left, right, (((0,), (0,)), ((), ())), preferred_element_type=jnp.float32
    )


def contract_cols(left, right):
    return lax.dot_general(
        left, right, (((1,), (1,)), ((), ())), preferred_element_type=jnp.float32
    )


def elementwise_step(summed, hidden_units):
    gate = summed[:, :hidden_units]
    up = summed[:, hidden_units : 2 * hidden_units]
    hidden_grad = summed[:, 2 * hidden_units :]
    sigmoid_gate = jax.nn.sigmoid(gate)
    activated = gate * sigmoid_gate
    hidden = (activated * up).astype(jnp.bfloat16)
    d_gate = (hidden_grad * up * sigmoid_gate * (1.0 + gate * (1.0 - sigmoid_gate))).astype(
        jnp.bfloat16
    )
    d_up = (hidden_grad * activated).astype(jnp.bfloat16)
    return (hidden, d_gate, d_up)


def on_device(stash, mlp_grad, qkv_grad, w_gate, w_up, w_down, w_qkv):
    rows_all, grads_all = (
        lax.all_gather(stash, ("gy", "gz"), axis=0, tiled=True),
        lax.all_gather(mlp_grad, ("gy", "gz"), axis=0, tiled=True),
    )
    qkv_all = lax.all_gather(qkv_grad, "gx", axis=0, tiled=True)
    hidden_units = w_gate.shape[1]
    gate_part = jnp.dot(rows_all, w_gate, preferred_element_type=jnp.float32)
    up_part = jnp.dot(rows_all, w_up, preferred_element_type=jnp.float32)
    back_part = contract_cols(grads_all, w_down)
    shares_sum = lax.psum_scatter(
        jnp.concatenate([gate_part, up_part, back_part], axis=1),
        "gx",
        scatter_dimension=0,
        tiled=True,
    )
    hidden_own, dgate_own, dup_own = elementwise_step(shares_sum, hidden_units)
    hidden, d_gate, d_up = (
        lax.all_gather(hidden_own, "gx", axis=0, tiled=True),
        lax.all_gather(dgate_own, "gx", axis=0, tiled=True),
        lax.all_gather(dup_own, "gx", axis=0, tiled=True),
    )
    grad_down = contract_rows(hidden, grads_all).astype(jnp.bfloat16)
    grad_gate = contract_rows(rows_all, d_gate).astype(jnp.bfloat16)
    grad_up = contract_rows(rows_all, d_up).astype(jnp.bfloat16)
    grad_qkv = contract_rows(rows_all, qkv_all).astype(jnp.bfloat16)
    result = contract_cols(d_gate, w_gate)
    result = result + contract_cols(d_up, w_up)
    grad_input = lax.psum_scatter(
        result + contract_cols(qkv_all, w_qkv), ("gy", "gz"), scatter_dimension=0, tiled=True
    ).astype(jnp.bfloat16)
    return (grad_input, grad_gate, grad_up, grad_down, grad_qkv)


def solution(mesh):
    return jax.shard_map(
        on_device,
        mesh=mesh,
        in_specs=(
            P(("gy", "gz"), "gx"),
            P(("gy", "gz"), "gx"),
            P("gx", ("gy", "gz")),
            P("gx", ("gy", "gz")),
            P("gx", ("gy", "gz")),
            P(("gy", "gz"), "gx"),
            P("gx", ("gy", "gz")),
        ),
        out_specs=(
            P(("gy", "gz"), "gx"),
            P("gx", ("gy", "gz")),
            P("gx", ("gy", "gz")),
            P(("gy", "gz"), "gx"),
            P("gx", ("gy", "gz")),
        ),
        check_vma=False,
    )
```

profile of v0, /device:TPU:1, one launch (start us, length us, event | category | flops | bytes accessed | tf_op | source)
XLA Modules:
  0.0 709.4 jit_solution(5661174397787786379)
XLA Ops:
  7.2 0.0 copy-start
  7.2 0.0 reduce-scatter.4.cloned.1.call-start
  7.2 144.2 %all-gather = bf16[64,10,768]{2,1,0:T(8,128)(2,1)} all-gather(bf16[1,10,768]{2,1,0:T(8,128)(2,1)} %bitcast.28), channel_id=1, replica_groups=mesh['gx'=8,'gy'=8,'gz'=8] {'gy','gz'}, dimensions={0}, use_global_device_ids=true | all-gather | bytes 998400 | tf_op jit(solution)/shard_map/all_gather | solution.py:35
  151.5 2.3 reshape.11
  153.8 0.5 fusion.4
  154.4 1.4 fusion.3
  155.7 139.9 %all-gather.1 = bf16[64,10,768]{2,1,0:T(8,128)(2,1)} all-gather(bf16[1,10,768]{2,1,0:T(8,128)(2,1)S(1)} %bitcast.29), channel_id=1, replica_groups=mesh['gx'=8,'gy'=8,'gz'=8] {'gy','gz'}, dimensions={0}, use_global_device_ids=true | all-gather | bytes 998400 | tf_op jit(solution)/shard_map/all_gather | solution.py:36
  295.6 2.3 reshape.13
  297.9 0.5 fusion.5
  298.4 0.6 copy-done.1
  299.0 1.4 pad_maximum_fusion
  300.4 2.8 copy.26
  303.2 0.0 reduce-scatter.4.cloned.1.call-update
  303.3 1.3 dynamic-slice
  305.2 21.6 %all_gather.22 = bf16[640,288]{1,0:T(8,128)(2,1)S(1)} all-gather(bf16[80,288]{1,0:T(8,128)(2,1)S(1)} %copy-done.7), channel_id=1, replica_groups=mesh['gx'=8,'gy'=8,'gz'=8] {'gx'}, dimensions={0}, use_global_device_ids=true | all-gather | bytes 414720 | tf_op jit(solution)/shard_map/all_gather | solution.py:38
  326.8 1.3 convolution_convert_fusion
  328.1 19.5 %reduce-scatter.4.cloned.1.call-done = f32[80,768]{1,0:T(8,128)} async-done(((f32[640,768]{1,0:T(8,128)}), f32[80,768]{1,0:T(8,128)}) %reduce-scatter.4.cloned.1.call-update) | async-done | bytes 245776 | tf_op jit(solution)/shard_map/reduce_scatter | solution.py:43
  347.6 1.0 multiply_convert_fusion
  348.6 19.4 %all_gather.21 = bf16[640,256]{1,0:T(8,128)(2,1)S(1)} all-gather(bf16[80,256]{1,0:T(8,128)(2,1)S(1)} %get-tuple-element.26), channel_id=1, replica_groups=mesh['gx'=8,'gy'=8,'gz'=8] {'gx'}, dimensions={0}, use_global_device_ids=true | all-gather | bytes 368640 | tf_op jit(solution)/shard_map/all_gather | solution.py:53
  368.0 0.5 fusion.1
  368.5 0.0 copy-start.5
  368.6 2.8 fusion.7
  371.3 18.5 %all_gather.20 = bf16[640,256]{1,0:T(8,128)(2,1)S(1)} all-gather(bf16[80,256]{1,0:T(8,128)(2,1)S(1)} %get-tuple-element.27), channel_id=1, replica_groups=mesh['gx'=8,'gy'=8,'gz'=8] {'gx'}, dimensions={0}, use_global_device_ids=true | all-gather | bytes 368640 | tf_op jit(solution)/shard_map/all_gather | solution.py:52
  389.8 1.3 fusion
  391.1 1.8 fusion.6
  392.9 19.0 %all_gather.23 = bf16[640,256]{1,0:T(8,128)(2,1)S(1)} all-gather(bf16[80,256]{1,0:T(8,128)(2,1)S(1)} %get-tuple-element.25), channel_id=1, replica_groups=mesh['gx'=8,'gy'=8,'gz'=8] {'gx'}, dimensions={0}, use_global_device_ids=true | all-gather | bytes 368640 | tf_op jit(solution)/shard_map/all_gather | solution.py:51
  411.8 1.3 convolution_convert_fusion.1
  413.1 0.9 copy.25
  414.0 0.9 copy.24
  414.9 2.8 add_add_fusion
  417.7 284.2 %all-reduce.2 = bf16[640,768]{1,0:T(8,128)(2,1)S(1)} all-reduce(f32[640,768]{1,0:T(8,128)S(1)} %add_add_fusion), channel_id=3, replica_groups=mesh['gx'=8,'gy'=8,'gz'=8] {'gy','gz'}, use_global_device_ids=true, to_apply=%region_1.0.clone | all-reduce | flops 491520 | bytes 2949120
  701.9 0.6 dynamic-slice_convert_fusion
  (15 shorter events, 0.0 us)
Async XLA Ops:
  7.2 407.8 %copy-start = (bf16[768,288]{0,1:T(8,128)(2,1)S(1)}, bf16[768,288]{0,1:T(8,128)(2,1)}, u32[]{:S(2)}) copy-start(bf16[768,288]{0,1:T(8,128)(2,1)} %param.13) | copy-start | bytes 1327108
  7.2 340.4 %reduce-scatter.4.cloned.1.call-start = ((), (), s32[]{:S(2)}) async-start(), calls=%async_computation.1 | async-start | bytes 2211840 | tf_op jit(solution)/shard_map/reduce_scatter | solution.py:43
  7.2 146.6 %copy-start.3 = (bf16[768,256]{1,0:T(8,128)(2,1)S(1)}, bf16[768,256]{1,0:T(8,128)(2,1)}, u32[]{:S(2)}) copy-start(bf16[768,256]{1,0:T(8,128)(2,1)} %param.11) | copy-start | bytes 1179652
  151.5 2.9 copy-start.4
  153.8 1.9 copy-start.8
  155.7 142.2 %copy-start.6 = (bf16[256,768]{1,0:T(8,128)(2,1)S(1)}, bf16[256,768]{1,0:T(8,128)(2,1)}, u32[]{:S(2)}) copy-start(bf16[256,768]{1,0:T(8,128)(2,1)} %param.12) | copy-start | bytes 1179652
  297.9 1.1 copy-start.1
  303.2 2.0 copy-start.7
  368.5 22.6 %copy-start.5 = (bf16[768,256]{1,0:T(8,128)(2,1)S(1)}, bf16[768,256]{1,0:T(8,128)(2,1)}, u32[]{:S(2)}) copy-start(bf16[768,256]{1,0:T(8,128)(2,1)} %param.10) | copy-start | bytes 1179652
  392.9 21.1 %copy-start.2 = (bf16[768,256]{0,1:T(8,128)(2,1)S(1)}, bf16[768,256]{0,1:T(8,128)(2,1)}, u32[]{:S(2)}) copy-start(bf16[768,256]{0,1:T(8,128)(2,1)} %fusion) | copy-start | bytes 1179652
Sparse Core Ops, SparseCore 0:
  303.4 44.1 reduce-scatter.3
where the time goes:
time: 716 us; the launch traced here: 709 us
  blocking collectives  647 us (90%)
  waiting for transfers between devices  19.5 us (3%)
  between operations  14.8 us (2%)
  matrix products  14.1 us (2%)
  local copies, waits for them, and re-layouts  11.8 us (2%)
    unnamed x1, blocking collectives  284 us
    all_gather x1, blocking collectives, on_device(): lax.all_gather(stash, ('gy', 'gz'), axis=0, tiled=True)  144 us
    all_gather x1, blocking collectives, on_device(): lax.all_gather(mlp_grad, ('gy', 'gz'), axis=0, tiled=True)  140 us
    all_gather x1, blocking collectives, on_device(): qkv_all = lax.all_gather(qkv_grad, 'gx', axis=0, tiled=True)  21.6 us
    reduce_scatter x1, waiting for transfers between devices, on_device(): lax.psum_scatter(jnp.concatenate([gate_part, up_part, back_part], axis=1)...  19.5 us
    all_gather x1, blocking collectives, on_device(): lax.all_gather(dup_own, 'gx', axis=0, tiled=True)  19.4 us
    all_gather x1, blocking collectives, on_device(): lax.all_gather(hidden_own, 'gx', axis=0, tiled=True)  19 us
    all_gather x1, blocking collectives, on_device(): lax.all_gather(dgate_own, 'gx', axis=0, tiled=True)  18.5 us
  transfers between devices with their start and end apart: 1, of which 1 were waited for; matrix products, arithmetic and copies ran while one was open for 0% of the time, Pallas kernels for 0%

commit v1 on v0

v1 whole, which is shorter than its diff:
```python
import jax
import jax.numpy as jnp
from jax import lax
from jax.experimental import pallas as pl
from jax.experimental.pallas import tpu as pltpu
from jax.sharding import PartitionSpec as P

MESH = pl.DeviceIdType.MESH
F32 = jnp.float32
BF16 = jnp.bfloat16
NY = 8
NS = 8
NH = 4
ROWS = 10
PAD = 16
BLK = 80
TB = 40
LANES = 128


def nt(left, right):
    return lax.dot_general(left, right, (((1,), (1,)), ((), ())), preferred_element_type=F32)


def tn(left, right):
    return lax.dot_general(left, right, (((0,), (0,)), ((), ())), preferred_element_type=F32)


def packing(shape, padded_dim):
    padded = lax.broadcasted_iota(jnp.int32, shape, padded_dim)
    packed = lax.broadcasted_iota(jnp.int32, shape, 1 - padded_dim)
    shard = lax.shift_right_logical(padded, 4)
    row = padded - shard * PAD
    return jnp.where((row < ROWS) & (packed == shard * ROWS + row), 1.0, 0.0).astype(BF16)


def kernel(
    stash, mlp, qkv, wg, wu, wd, wq,
    gi_out, gg_out, gu_out, gd_out, gq_out,
    pad, zin, shards, xs, xm, q, pf, sb, rb, ab, hid, dg, du, gif, cr, rs1, rr1, z2, zr,
    z_ss, z_rs, g_ss, g_rs, x_ss, x_rs, q_ss, q_rs, s_ss, s_rs, a_ss, a_rs, c_ss, c_rs, r_ss, r_rs, e_ss, e_rs,
):
    y = lax.axis_index("gx")
    gy = lax.axis_index("gy")
    s = lax.axis_index("gz")
    core, hi = gy % 2, gy // 2
    lo, x = s // 4, s % 4

    def at_y(d):
        return ((y + d) % NY, gy, s)

    def shard_peer(r):
        return ((lo + r // 4) % 2) * 4 + (x + r % 4) % 4

    def at_s(r):
        return (y, gy, shard_peer(r))

    def at_hi(k):
        return (y, ((hi + k + NH) % NH) * 2 + core, s)

    sibling = (y, hi * 2 + (1 - core), s)

    sends = []

    def send(src, dst, ss, rs, device):
        copy = pltpu.make_async_remote_copy(
            src_ref=src, dst_ref=dst, send_sem=ss, recv_sem=rs, device_id=device, device_id_type=MESH
        )
        copy.start()
        sends.append(copy)
        return copy

    pad[...] = jnp.zeros_like(pad)
    pad[0:ROWS, :] = stash[...]
    pad[PAD : PAD + ROWS, :] = mlp[...]
    shards[0, s] = pad[...]
    q[y] = qkv[...]

    barrier = pltpu.get_barrier_semaphore()
    partners = [at_y(d) for d in range(1, NY)] + [at_s(r) for r in range(1, NS)]
    partners += [at_hi(k) for k in range(1, NH)] + [sibling]
    for device in partners:
        pl.semaphore_signal(barrier, inc=1, device_id=device, device_id_type=MESH)
    pl.semaphore_wait(barrier, len(partners))

    def spread(k, src):
        return [
            send(src, shards.at[k, s], g_ss.at[k, r], g_rs.at[k, r], at_s(r))
            for r in (6, 2, 5, 7, 1, 3, 4)
        ]

    shard_copies = {0: spread(0, pad)}
    z_copies = {
        k: send(pad, zin.at[k], z_ss.at[k], z_rs.at[k], at_hi(-k)) for k in (2, 1, 3)
    }
    q_copies = [send(qkv, q.at[y], q_ss.at[d], q_rs.at[d], at_y(d)) for d in (4, 3, 5, 2, 6, 1, 7)]

    def group(k):
        return ((hi + k) % NH) * 2

    def forward_shard(k):
        z_copies[k].wait_recv()
        shard_copies[k] = spread(k, zin.at[k])
        shards[k, s] = zin[k]

    swaps = {}

    def gather_rows(k):
        for copy in shard_copies[k]:
            copy.wait_recv()
        pack = packing((BLK, NS * PAD), 1)
        block = group(k) + core
        for i, out in enumerate((xs, xm)):
            rows = shards[k, :, i * PAD : (i + 1) * PAD, :].reshape(NS * PAD, -1)
            out[block] = jnp.dot(pack, rows, preferred_element_type=F32).astype(BF16)
        swaps[k] = [
            send(out.at[block], out.at[block], x_ss.at[k, i], x_rs.at[k, i], sibling)
            for i, out in enumerate((xs, xm))
        ]

    sums = {}

    def project(k):
        for copy in swaps[k]:
            copy.wait_recv()
        rows = xs[pl.ds(group(k), 2)].reshape(2 * BLK, -1)
        grads = xm[pl.ds(group(k), 2)].reshape(2 * BLK, -1)
        gate = jnp.dot(rows, wg[...], preferred_element_type=F32)
        up = jnp.dot(rows, wu[...], preferred_element_type=F32)
        back = nt(grads, wd[...])
        for owner in range(NY):
            tb, ch = owner // 2, owner % 2
            part = jnp.concatenate(
                [
                    a[tb * TB : (tb + 1) * TB, ch * LANES : (ch + 1) * LANES]
                    for a in (gate, up, back)
                ]
                + [jnp.zeros((LANES - 3 * TB, LANES), F32)],
                axis=0,
            )
            pf[k, owner] = part
            sb[k, owner] = part.astype(BF16)
        sums[k] = [
            send(sb.at[k, (y + d) % NY], rb.at[k, d], s_ss.at[k, d], s_rs.at[k, d], at_y(d))
            for d in (4, 3, 5, 2, 6, 1, 7)
        ]

    results = {}

    def elementwise(k):
        total = pf[k, y]
        for copy in sums[k]:
            copy.wait_recv()
        for d in range(1, NY):
            total = total + rb[k, d].astype(F32)
        gate, up, back = total[0:TB], total[TB : 2 * TB], total[2 * TB : 3 * TB]
        sig = jax.nn.sigmoid(gate)
        act = gate * sig
        out = jnp.concatenate(
            [
                act * up,
                back * up * sig * (1.0 + gate * (1.0 - sig)),
                back * act,
                jnp.zeros((LANES - 3 * TB, LANES), F32),
            ],
            axis=0,
        )
        ab[k, y] = out.astype(BF16)
        results[k] = [
            send(ab.at[k, y], ab.at[k, y], a_ss.at[k, d], a_rs.at[k, d], at_y(d))
            for d in (4, 3, 5, 2, 6, 1, 7)
        ]

    halves = {}

    def input_partial(k):
        for copy in results[k]:
            copy.wait_recv()
        if k == 0:
            for copy in q_copies:
                copy.wait_recv()
        for b in range(2):
            for ch in range(2):
                first = ab[k, 4 * b + ch].astype(F32)
                second = ab[k, 4 * b + 2 + ch].astype(F32)
                for i, out in enumerate((hid, dg, du)):
                    out[group(k) + b, :, ch * LANES : (ch + 1) * LANES] = jnp.concatenate(
                        [first[i * TB : (i + 1) * TB], second[i * TB : (i + 1) * TB]], axis=0
                    ).astype(BF16)
        blocks = pl.ds(group(k), 2)
        part = nt(dg[blocks].reshape(2 * BLK, -1), wg[...])
        part += nt(du[blocks].reshape(2 * BLK, -1), wu[...])
        part += nt(q[blocks].reshape(2 * BLK, -1), wq[...])
        gif[k] = part.reshape(2, BLK, -1)
        halves[k] = send(gif.at[k, 1 - core], cr.at[k], c_ss.at[k], c_rs.at[k], sibling)

    pieces = {}

    def scatter_input(k):
        halves[k].wait_recv()
        block = (gif[k, core] + cr[k]).astype(BF16)
        unpack = packing((NS * PAD, BLK), 0)
        rs1[k] = (
            jnp.dot(unpack, block, preferred_element_type=F32).astype(BF16).reshape(NS, PAD, -1)
        )
        pieces[k] = [
            send(rs1.at[k, shard_peer(r)], rr1.at[k, r], r_ss.at[k, r], r_rs.at[k, r], at_s(r))
            for r in (6, 2, 5, 7, 1, 3, 4)
        ]

    ends = []

    def reduce_input(k):
        total = rs1[k, s].astype(F32)
        for copy in pieces[k]:
            copy.wait_recv()
        for r in range(1, NS):
            total = total + rr1[k, r].astype(F32)
        z2[k] = total
        if k > 0:
            ends.append(send(z2.at[k], zr.at[k], e_ss.at[k], e_rs.at[k], at_hi(k)))

    def flat(ref):
        return ref[...].reshape(NY * BLK, -1)

    forward_shard(1)
    gather_rows(0)
    forward_shard(2)
    project(0)
    forward_shard(3)
    gather_rows(1)
    project(1)
    elementwise(0)
    gather_rows(2)
    project(2)
    elementwise(1)
    gather_rows(3)
    project(3)
    input_partial(0)
    elementwise(2)
    scatter_input(0)
    input_partial(1)
    elementwise(3)
    scatter_input(1)
    reduce_input(0)
    input_partial(2)
    scatter_input(2)
    reduce_input(1)
    input_partial(3)
    scatter_input(3)
    reduce_input(2)
    gg_out[...] = tn(flat(xs), flat(dg)).astype(BF16)
    gu_out[...] = tn(flat(xs), flat(du)).astype(BF16)
    reduce_input(3)
    gd_out[...] = tn(flat(hid), flat(xm)).astype(BF16)
    gq_out[...] = tn(flat(xs), flat(q)).astype(BF16)
    total = z2[0]
    for copy in ends:
        copy.wait_recv()
    for k in range(1, NH):
        total = total + zr[k]
    gi_out[...] = total[0:ROWS].astype(BF16)
    for copy in sends:
        copy.wait_send()


def on_device(stash, mlp_grad, qkv_grad, w_gate, w_up, w_down, w_qkv):
    width = stash.shape[1]
    units = w_gate.shape[1]
    proj = w_qkv.shape[1]
    vmem = pl.BlockSpec(memory_space=pltpu.VMEM)
    dma = pltpu.SemaphoreType.DMA
    return pl.pallas_call(
        kernel,
        out_shape=(
            jax.ShapeDtypeStruct(stash.shape, BF16),
            jax.ShapeDtypeStruct(w_gate.shape, BF16),
            jax.ShapeDtypeStruct(w_up.shape, BF16),
            jax.ShapeDtypeStruct(w_down.shape, BF16),
            jax.ShapeDtypeStruct(w_qkv.shape, BF16),
        ),
        in_specs=[vmem] * 7,
        out_specs=(vmem,) * 5,
        scratch_shapes=[
            pltpu.VMEM((2 * PAD, width), BF16),
            pltpu.VMEM((NH, 2 * PAD, width), BF16),
            pltpu.VMEM((NH, NS, 2 * PAD, width), BF16),
            pltpu.VMEM((NY, BLK, width), BF16),
            pltpu.VMEM((NY, BLK, width), BF16),
            pltpu.VMEM((NY, BLK, proj), BF16),
            pltpu.VMEM((NH, NY, LANES, LANES), F32),
            pltpu.VMEM((NH, NY, LANES, LANES), BF16),
            pltpu.VMEM((NH, NY, LANES, LANES), BF16),
            pltpu.VMEM((NH, NY, LANES, LANES), BF16),
            pltpu.VMEM((NY, BLK, units), BF16),
            pltpu.VMEM((NY, BLK, units), BF16),
            pltpu.VMEM((NY, BLK, units), BF16),
            pltpu.VMEM((NH, 2, BLK, width), F32),
            pltpu.VMEM((NH, BLK, width), F32),
            pltpu.VMEM((NH, NS, PAD, width), BF16),
            pltpu.VMEM((NH, NS, PAD, width), BF16),
            pltpu.VMEM((NH, PAD, width), F32),
            pltpu.VMEM((NH, PAD, width), F32),
        ]
        + [dma((NH,))] * 2
        + [dma((NH, NS))] * 2
        + [dma((NH, 2))] * 2
        + [dma((NY,))] * 2
        + [dma((NH, NY))] * 2
        + [dma((NH, NY))] * 2
        + [dma((NH,))] * 2
        + [dma((NH, NS))] * 2
        + [dma((NH,))] * 2,
        compiler_params=pltpu.CompilerParams(
            collective_id=0, has_side_effects=True, vmem_limit_bytes=44 * 2**20
        ),
        cost_estimate=pl.CostEstimate(
            flops=2_600_000_000, bytes_accessed=4_000_000, transcendentals=200_000
        ),
        name="block_backward",
    )(stash, mlp_grad, qkv_grad, w_gate, w_up, w_down, w_qkv)


def solution(mesh):
    rows = P(("gy", "gz"), "gx")
    columns = P("gx", ("gy", "gz"))
    return jax.shard_map(
        on_device,
        mesh=mesh,
        in_specs=(rows, rows, columns, columns, columns, rows, columns),
        out_specs=(rows, columns, columns, rows, columns),
        check_vma=False,
    )
```

time: 716 us -> 97.2 us (0.14)
  the two profiles are of different devices: /device:TPU:1 before, /device:TPU:16 now
where the time goes in v1:
time: 97.2 us; the launch traced here: 97 us
  Pallas kernels  90 us (93%)
  local copies, waits for them, and re-layouts  6.23 us (6%)
    pallas_call x1, Pallas kernels, on_device(): pl.pallas_call(kernel, out_shape=(jax.ShapeDtypeStruct(stash.shape, BF16)...  90 us
    unnamed x17, local copies, waits for them, and re-layouts  5.24 us

profile of v1, /device:TPU:16, one launch (start us, length us, event | category | flops | bytes accessed | tf_op | source)
XLA Modules:
  0.0 97.0 jit_solution(14979496085670707962)
XLA Ops:
  0.6 0.0 copy-start.1
  0.6 0.0 copy-start
  0.7 0.0 copy-start.3
  0.7 0.0 copy-start.5
  0.7 0.0 copy-start.4
  0.7 1.4 %copy.12.wq = bf16[768,288]{1,0:T(8,128)(2,1)S(1)} copy(bf16[768,288]{0,1:T(8,128)(2,1)} %param.13) | data formatting | bytes 884736 | tf_op args[6]
  2.1 0.0 copy-done.1
  2.1 0.0 copy-done
  2.1 0.0 copy-done.3
  2.1 0.0 copy-done.5
  2.1 0.0 copy-done.4
  2.1 0.0 copy-start.2
  2.1 1.0 %copy-done.2 = bf16[256,768]{1,0:T(8,128)(2,1)S(1)} copy-done((bf16[256,768]{1,0:T(8,128)(2,1)S(1)}, bf16[256,768]{1,0:T(8,128)(2,1)}, u32[]{:S(2)}) %copy-start.2) | copy-done | bytes 393240
  3.1 90.0 %block_backward.1 = (bf16[10,768]{1,0:T(8,128)(2,1)S(1)}, bf16[768,256]{1,0:T(8,128)(2,1)S(1)}, bf16[768,256]{1,0:T(8,128)(2,1)S(1)}, bf16[256,768]{1,0:T(8,128)(2,1)S(1)}, bf16[768,288]{1,0:T(8,128)(2,1)S(1)}) custom-call(bf16[10,768]{1,0:T(8,128)(2,1)S(1)} %copy-done.4, bf16[10,768]{1,0:T(8,128)(2,1)S(1)} %copy-done.5, bf16[80,288]{1,0:T(8,128)(2,1)S(1)} %copy-done.3, ...), custom_call_target="tpu_custom_call" | custom-call | flops 2600000000 | bytes 4000000 | tf_op jit(solution)/shard_map/block_backward/pallas_call | solution.py:273
  93.1 1.0 %copy.13 = bf16[768,288]{0,1:T(8,128)(2,1)} copy(bf16[768,288]{1,0:T(8,128)(2,1)S(1)} %get-tuple-element.9) | data formatting | bytes 884736 | tf_op jit(solution)/shard_map/block_backward/pallas_call | solution.py:273
  94.1 0.6 copy.18
  94.7 0.7 copy.19
  95.5 0.7 copy.20
  96.2 0.7 copy.21
Async XLA Ops:
  0.6 1.4 %copy-start.1 = (bf16[768,256]{1,0:T(8,128)(2,1)S(1)}, bf16[768,256]{1,0:T(8,128)(2,1)}, u32[]{:S(2)}) copy-start(bf16[768,256]{1,0:T(8,128)(2,1)} %wu.1) | copy-start | bytes 1179652
  0.6 1.4 %copy-start = (bf16[768,256]{1,0:T(8,128)(2,1)S(1)}, bf16[768,256]{1,0:T(8,128)(2,1)}, u32[]{:S(2)}) copy-start(bf16[768,256]{1,0:T(8,128)(2,1)} %wg.1) | copy-start | bytes 1179652
  0.7 1.4 %copy-start.3 = (bf16[80,288]{1,0:T(8,128)(2,1)S(1)}, bf16[80,288]{1,0:T(8,128)(2,1)}, u32[]{:S(2)}) copy-start(bf16[80,288]{1,0:T(8,128)(2,1)} %qkv.1) | copy-start | bytes 138244
  0.7 1.4 %copy-start.5 = (bf16[10,768]{1,0:T(8,128)(2,1)S(1)}, bf16[10,768]{1,0:T(8,128)(2,1)}, u32[]{:S(2)}) copy-start(bf16[10,768]{1,0:T(8,128)(2,1)} %mlp.1) | copy-start | bytes 46084
  0.7 1.4 %copy-start.4 = (bf16[10,768]{1,0:T(8,128)(2,1)S(1)}, bf16[10,768]{1,0:T(8,128)(2,1)}, u32[]{:S(2)}) copy-start(bf16[10,768]{1,0:T(8,128)(2,1)} %stash.1) | copy-start | bytes 46084
  2.1 1.0 %copy-start.2 = (bf16[256,768]{1,0:T(8,128)(2,1)S(1)}, bf16[256,768]{1,0:T(8,128)(2,1)}, u32[]{:S(2)}) copy-start(bf16[256,768]{1,0:T(8,128)(2,1)} %wd.1) | copy-start | bytes 1179652

commit v2 on v1

v2 whole, which is shorter than its diff:
```python
import jax
import jax.numpy as jnp
from jax import lax
from jax.experimental import pallas as pl
from jax.experimental.pallas import tpu as pltpu
from jax.sharding import PartitionSpec as P

MESH = pl.DeviceIdType.MESH
F32 = jnp.float32
BF16 = jnp.bfloat16
NY = 8
NS = 8
NH = 4
ROWS = 10
PAD = 16
BLK = 80
TB = 40
LANES = 128


def nt(left, right):
    return lax.dot_general(left, right, (((1,), (1,)), ((), ())), preferred_element_type=F32)


def tn(left, right):
    return lax.dot_general(left, right, (((0,), (0,)), ((), ())), preferred_element_type=F32)


def one_hot(rows, cols, hit):
    row = lax.broadcasted_iota(jnp.int32, (rows, cols), 0)
    col = lax.broadcasted_iota(jnp.int32, (rows, cols), 1)
    return jnp.where(hit(row, col), 1.0, 0.0).astype(BF16)


def spreading(row, col):
    shard = lax.shift_right_logical(row, 4)
    token = row - shard * PAD
    return (token < ROWS) & (col == shard * ROWS + token)


def exact(left, right):
    return jnp.dot(left, right, preferred_element_type=F32)


HEAD = PAD - ROWS
TAIL = ROWS - HEAD


def pack_shard(padded, width):
    main = one_hot(PAD, 2 * PAD, lambda r, c: ((r < ROWS) & (c == r)) | ((r >= ROWS) & (c == r + HEAD)))
    parts = [exact(main, padded)]
    for half in range(2):
        part = jnp.zeros((PAD, LANES), F32)
        for i in range(4 * half, min(4 * half + 4, width // LANES)):
            low = TAIL * (i % 4)
            pick = one_hot(
                PAD, 2 * PAD, lambda r, c: (r >= low) & (r < low + TAIL) & (c == r - low + PAD + HEAD)
            )
            part += exact(pick, padded[:, i * LANES : (i + 1) * LANES])
        parts.append(part)
    return jnp.concatenate(parts, axis=1).astype(BF16)


def unpack_shards(packed, width):
    def place(row, col, low, count, start):
        shard = lax.shift_right_logical(col, 4)
        t = col - shard * PAD - low
        return (t >= 0) & (t < count) & (row == shard * ROWS + start + t)

    wide = packed[:, :width]
    rows = exact(one_hot(BLK, NS * PAD, lambda r, c: place(r, c, 0, ROWS, 0)), wide)
    grads = exact(one_hot(BLK, NS * PAD, lambda r, c: place(r, c, ROWS, HEAD, 0)), wide)
    tails = []
    for i in range(width // LANES):
        pick = one_hot(BLK, NS * PAD, lambda r, c: place(r, c, TAIL * (i % 4), TAIL, HEAD))
        first = width + LANES * (i // 4)
        tails.append(exact(pick, packed[:, first : first + LANES]))
    grads += jnp.concatenate(tails, axis=1)
    return rows.astype(BF16), grads.astype(BF16)


def kernel(
    stash_in, mlp_in, qkv_in, wg_in, wu_in, wd_in, wq_in,
    gi_out, gg_out, gu_out, gd_out, gq_out,
    stash, mlp, qkv, wg, wu, wd, wq,
    pad, packed, zin, shards, xs, xm, q, pf, sb, rb, cb, ab, hid, dg, du, gif, cr, rs1, rr1, own, z2, zr,
    w_sem, z_ss, z_rs, g_ss, g_rs, x_ss, x_rs, q_ss, q_rs, s_ss, s_rs, a_ss, a_rs, c_ss, c_rs, r_ss, r_rs, e_ss, e_rs,
):
    y = lax.axis_index("gx")
    gy = lax.axis_index("gy")
    s = lax.axis_index("gz")
    core, hi = gy % 2, gy // 2
    lo, x = s // 4, s % 4

    def at_y(d):
        return ((y + d + NY) % NY, gy, s)

    def shard_peer(r):
        return ((lo + r // 4) % 2) * 4 + (x + r % 4) % 4

    def at_s(r):
        return (y, gy, shard_peer(r))

    def at_hi(k):
        return (y, ((hi + k + NH) % NH) * 2 + core, s)

    sibling = (y, hi * 2 + (1 - core), s)

    sends = []

    def send(src, dst, ss, rs, device):
        copy = pltpu.make_async_remote_copy(
            src_ref=src, dst_ref=dst, send_sem=ss, recv_sem=rs, device_id=device, device_id_type=MESH
        )
        copy.start()
        sends.append(copy)
        return copy

    inputs = [
        pltpu.make_async_copy(src, dst, w_sem.at[i])
        for i, (src, dst) in enumerate(
            (
                (stash_in, stash),
                (mlp_in, mlp),
                (qkv_in, qkv),
                (wg_in, wg),
                (wu_in, wu),
                (wd_in, wd),
                (wq_in, wq),
            )
        )
    ]
    for copy in inputs:
        copy.start()
    barrier = pltpu.get_barrier_semaphore()
    partners = [at_y(d) for d in (1, -1, 2, -2)] + [at_s(r) for r in range(1, NS)]
    partners += [at_hi(k) for k in range(1, NH)] + [sibling]
    for device in partners:
        pl.semaphore_signal(barrier, inc=1, device_id=device, device_id_type=MESH)

    for copy in inputs[:3]:
        copy.wait()
    pad[...] = jnp.zeros_like(pad)
    pad[0:ROWS, :] = stash[...]
    pad[PAD : PAD + ROWS, :] = mlp[...]
    packed[...] = pack_shard(pad[...], stash.shape[1])
    shards[0, s] = packed[...]
    q[y] = qkv[...]

    pl.semaphore_wait(barrier, len(partners))

    def spread(k, src):
        return [
            send(src, shards.at[k, s], g_ss.at[k, r], g_rs.at[k, r], at_s(r))
            for r in (6, 2, 5, 7, 1, 3, 4)
        ]

    shard_copies = {0: spread(0, packed)}
    z_copies = {
        k: send(packed, zin.at[k], z_ss.at[k], z_rs.at[k], at_hi(-k)) for k in (2, 1, 3)
    }

    def wrap(d):
        return (y + d + NY) % NY

    def share(ref, ss, rs):
        block = ref.at[y]
        return {
            d: send(block, block, ss.at[i], rs.at[i], at_y(-d))
            for i, d in enumerate((2, -2, 1, -1))
        }

    def pass_on(copies, ref, ss, rs, cut):
        halves = {2: pl.ds(0, cut), -2: pl.ds(cut, ref.shape[1] - cut)}
        for i, d in enumerate((2, -2)):
            copies[d].wait_recv()
            block = ref.at[wrap(d)]
            part = ref.at[wrap(d), halves[d]]
            sign = d // 2
            copies[2 * d] = send(part, part, ss.at[4 + i], rs.at[4 + i], at_y(-d))
            copies[d + sign] = send(block, block, ss.at[6 + i], rs.at[6 + i], at_y(-sign))

    def shared(copies):
        for d in (1, -1, 3, -3, 4, -4):
            copies[d].wait_recv()

    q_copies = share(q, q_ss, q_rs)

    def pass_q():
        pass_on(q_copies, q, q_ss, q_rs, 48)

    def group(k):
        return ((hi + k) % NH) * 2

    def forward_shard(k):
        z_copies[k].wait_recv()
        shard_copies[k] = spread(k, zin.at[k])
        shards[k, s] = zin[k]

    swaps = {}

    def gather_rows(k):
        for copy in shard_copies[k]:
            copy.wait_recv()
        block = group(k) + core
        xs[block], xm[block] = unpack_shards(shards[k].reshape(NS * PAD, -1), stash.shape[1])
        swaps[k] = [
            send(out.at[block], out.at[block], x_ss.at[k, i], x_rs.at[k, i], sibling)
            for i, out in enumerate((xs, xm))
        ]

    sums = {}

    def project(k):
        for copy in swaps[k]:
            copy.wait_recv()
        if k == 0:
            for copy in inputs[3:6]:
                copy.wait()
        rows = xs[pl.ds(group(k), 2)].reshape(2 * BLK, -1)
        grads = xm[pl.ds(group(k), 2)].reshape(2 * BLK, -1)
        gate = jnp.dot(rows, wg[...], preferred_element_type=F32)
        up = jnp.dot(rows, wu[...], preferred_element_type=F32)
        back = nt(grads, wd[...])
        for owner in range(NY):
            tb, ch = owner // 2, owner % 2
            part = jnp.concatenate(
                [
                    a[tb * TB : (tb + 1) * TB, ch * LANES : (ch + 1) * LANES]
                    for a in (gate, up, back)
                ]
                + [jnp.zeros((LANES - 3 * TB, LANES), F32)],
                axis=0,
            )
            pf[k, owner] = part
            sb[k, owner] = part.astype(BF16)
        half = {1: pl.ds(0, LANES // 2), -1: pl.ds(LANES // 2, LANES // 2)}
        sums[k] = {}
        for slot, (dist, hop) in enumerate(((4, 2), (3, 1), (1, 1))):
            for side, sign in enumerate((1, -1)):
                src = sb.at[k, wrap(sign * dist)]
                dst = rb.at[k, 2 * slot + side]
                if dist == 4:
                    src = sb.at[k, wrap(sign * dist), half[sign]]
                    dst = rb.at[k, 2 * slot + side, half[sign]]
                n = 2 * slot + side
                sums[k][dist, sign] = send(src, dst, s_ss.at[k, n], s_rs.at[k, n], at_y(sign * hop))

    def combine(k):
        for side, sign in enumerate((1, -1)):
            sums[k][4, sign].wait_recv()
            sums[k][3, sign].wait_recv()
            rows = LANES // 2 * side
            part = pf[k, wrap(2 * sign)] + rb[k, 2 + side].astype(F32)
            far = rb[k, side, rows : rows + LANES // 2, :].astype(F32)
            blank = jnp.zeros_like(far)
            part += jnp.concatenate([far, blank] if side == 0 else [blank, far], axis=0)
            cb[k, side] = part.astype(BF16)
            sums[k][2, sign] = send(
                cb.at[k, side], rb.at[k, 6 + side], s_ss.at[k, 6 + side], s_rs.at[k, 6 + side], at_y(2 * sign)
            )

    results = {}

    def elementwise(k):
        total = pf[k, y]
        for slot, dist in ((2, 1), (3, 2)):
            for side, sign in enumerate((1, -1)):
                sums[k][dist, sign].wait_recv()
                total = total + rb[k, 2 * slot + side].astype(F32)
        gate, up, back = total[0:TB], total[TB : 2 * TB], total[2 * TB : 3 * TB]
        sig = jax.nn.sigmoid(gate)
        act = gate * sig
        out = jnp.concatenate(
            [
                act * up,
                back * up * sig * (1.0 + gate * (1.0 - sig)),
                back * act,
                jnp.zeros((LANES - 3 * TB, LANES), F32),
            ],
            axis=0,
        )
        ab[k, y] = out.astype(BF16)
        results[k] = share(ab.at[k], a_ss.at[k], a_rs.at[k])

    def pass_results(k):
        pass_on(results[k], ab.at[k], a_ss.at[k], a_rs.at[k], LANES // 2)

    halves = {}

    def input_partial(k):
        shared(results[k])
        if k == 0:
            shared(q_copies)
            inputs[6].wait()
        for b in range(2):
            for ch in range(2):
                first = ab[k, 4 * b + ch].astype(F32)
                second = ab[k, 4 * b + 2 + ch].astype(F32)
                for i, out in enumerate((hid, dg, du)):
                    out[group(k) + b, :, ch * LANES : (ch + 1) * LANES] = jnp.concatenate(
                        [first[i * TB : (i + 1) * TB], second[i * TB : (i + 1) * TB]], axis=0
                    ).astype(BF16)
        def partial(block):
            part = nt(dg[block], wg[...])
            part += nt(du[block], wu[...])
            part += jnp.dot(q[block], wq[...], preferred_element_type=F32)
            return part

        gif[k, 1] = partial(group(k) + 1 - core)
        halves[k] = send(gif.at[k, 1], cr.at[k], c_ss.at[k], c_rs.at[k], sibling)
        gif[k, 0] = partial(group(k) + core)

    pieces = {}

    def scatter_input(k):
        halves[k].wait_recv()
        block = (gif[k, 0] + cr[k]).astype(BF16)
        unpack = one_hot(NS * PAD, BLK, spreading)
        rs1[k] = (
            jnp.dot(unpack, block, preferred_element_type=F32).astype(BF16).reshape(NS, PAD, -1)
        )
        pieces[k] = [
            send(rs1.at[k, shard_peer(r)], rr1.at[k, r], r_ss.at[k, r], r_rs.at[k, r], at_s(r))
            for r in (6, 2, 5, 7, 1, 3, 4)
        ]

    ends = []

    def reduce_input(k):
        total = rs1[k, s].astype(F32)
        for copy in pieces[k]:
            copy.wait_recv()
        for r in range(1, NS):
            total = total + rr1[k, r].astype(F32)
        if k == 0:
            own[...] = total
        else:
            z2[k] = total.astype(BF16)
            ends.append(send(z2.at[k], zr.at[k], e_ss.at[k], e_rs.at[k], at_hi(k)))

    def flat(ref):
        return ref[...].reshape(NY * BLK, -1)

    gather_rows(0)
    forward_shard(1)
    pass_q()
    project(0)
    forward_shard(2)
    gather_rows(1)
    combine(0)
    project(1)
    forward_shard(3)
    elementwise(0)
    combine(1)
    gather_rows(2)
    project(2)
    pass_results(0)
    elementwise(1)
    combine(2)
    gather_rows(3)
    project(3)
    input_partial(0)
    pass_results(1)
    elementwise(2)
    combine(3)
    scatter_input(0)
    input_partial(1)
    pass_results(2)
    elementwise(3)
    scatter_input(1)
    reduce_input(0)
    input_partial(2)
    pass_results(3)
    scatter_input(2)
    reduce_input(1)
    input_partial(3)
    scatter_input(3)
    reduce_input(2)
    gg_out[...] = tn(flat(xs), flat(dg)).astype(BF16)
    gu_out[...] = tn(flat(xs), flat(du)).astype(BF16)
    reduce_input(3)
    gd_out[...] = tn(flat(hid), flat(xm)).astype(BF16)
    gq_out[...] = tn(flat(q), flat(xs)).astype(BF16)
    total = own[...]
    for copy in ends:
        copy.wait_recv()
    for k in range(1, NH):
        total = total + zr[k].astype(F32)
    gi_out[...] = total[0:ROWS].astype(BF16)
    for copy in sends:
        copy.wait_send()


def place(*refs):
    ins, outs, held = refs[:5], refs[5:10], refs[10:15]
    in_sems, out_sems = refs[15:]
    loads = [pltpu.make_async_copy(ins[i], held[i], in_sems.at[i]) for i in range(5)]
    stores = [pltpu.make_async_copy(held[i], outs[i], out_sems.at[i]) for i in range(5)]
    for copy in loads:
        copy.start()
    for load, store in zip(loads, stores):
        load.wait()
        store.start()
    for copy in stores:
        copy.wait()


def on_device(stash, mlp_grad, qkv_grad, w_gate, w_up, w_down, w_qkv):
    width = stash.shape[1]
    units = w_gate.shape[1]
    proj = w_qkv.shape[1]
    vmem = pl.BlockSpec(memory_space=pltpu.VMEM)
    hbm = pl.BlockSpec(memory_space=pltpu.HBM)
    dma = pltpu.SemaphoreType.DMA
    results = pl.pallas_call(
        kernel,
        out_shape=(
            jax.ShapeDtypeStruct(stash.shape, BF16),
            jax.ShapeDtypeStruct(w_gate.shape, BF16),
            jax.ShapeDtypeStruct(w_up.shape, BF16),
            jax.ShapeDtypeStruct(w_down.shape, BF16),
            jax.ShapeDtypeStruct((proj, width), BF16),
        ),
        in_specs=[hbm] * 7,
        out_specs=(vmem,) * 5,
        scratch_shapes=[
            pltpu.VMEM(stash.shape, BF16),
            pltpu.VMEM(mlp_grad.shape, BF16),
            pltpu.VMEM(qkv_grad.shape, BF16),
            pltpu.VMEM(w_gate.shape, BF16),
            pltpu.VMEM(w_up.shape, BF16),
            pltpu.VMEM(w_down.shape, BF16),
            pltpu.VMEM((proj, width), BF16),
            pltpu.VMEM((2 * PAD, width), BF16),
            pltpu.VMEM((PAD, width + 2 * LANES), BF16),
            pltpu.VMEM((NH, PAD, width + 2 * LANES), BF16),
            pltpu.VMEM((NH, NS, PAD, width + 2 * LANES), BF16),
            pltpu.VMEM((NY, BLK, width), BF16),
            pltpu.VMEM((NY, BLK, width), BF16),
            pltpu.VMEM((NY, BLK, proj), BF16),
            pltpu.VMEM((NH, NY, LANES, LANES), F32),
            pltpu.VMEM((NH, NY, LANES, LANES), BF16),
            pltpu.VMEM((NH, NY, LANES, LANES), BF16),
            pltpu.VMEM((NH, 2, LANES, LANES), BF16),
            pltpu.VMEM((NH, NY, LANES, LANES), BF16),
            pltpu.VMEM((NY, BLK, units), BF16),
            pltpu.VMEM((NY, BLK, units), BF16),
            pltpu.VMEM((NY, BLK, units), BF16),
            pltpu.VMEM((NH, 2, BLK, width), F32),
            pltpu.VMEM((NH, BLK, width), F32),
            pltpu.VMEM((NH, NS, PAD, width), BF16),
            pltpu.VMEM((NH, NS, PAD, width), BF16),
            pltpu.VMEM((PAD, width), F32),
            pltpu.VMEM((NH, PAD, width), BF16),
            pltpu.VMEM((NH, PAD, width), BF16),
        ]
        + [dma((7,))]
        + [dma((NH,))] * 2
        + [dma((NH, NS))] * 2
        + [dma((NH, 2))] * 2
        + [dma((NY,))] * 2
        + [dma((NH, NY))] * 2
        + [dma((NH, NY))] * 2
        + [dma((NH,))] * 2
        + [dma((NH, NS))] * 2
        + [dma((NH,))] * 2,
        compiler_params=pltpu.CompilerParams(
            collective_id=0, has_side_effects=True, vmem_limit_bytes=63 * 2**20
        ),
        cost_estimate=pl.CostEstimate(
            flops=2_600_000_000, bytes_accessed=4_000_000, transcendentals=200_000
        ),
        name="block_backward",
    )(stash, mlp_grad, qkv_grad, w_gate, w_up, w_down, w_qkv.T)
    *placed, grad_qkv = pl.pallas_call(
        place,
        out_shape=tuple(jax.ShapeDtypeStruct(a.shape, a.dtype) for a in results),
        in_specs=[hbm] * 5,
        out_specs=(hbm,) * 5,
        scratch_shapes=[pltpu.VMEM(a.shape, a.dtype) for a in results] + [dma((5,))] * 2,
        compiler_params=pltpu.CompilerParams(vmem_limit_bytes=63 * 2**20),
        name="place_results",
    )(*results)
    return (*placed, grad_qkv.T)


def solution(mesh):
    rows = P(("gy", "gz"), "gx")
    columns = P("gx", ("gy", "gz"))
    return jax.shard_map(
        on_device,
        mesh=mesh,
        in_specs=(rows, rows, columns, columns, columns, rows, columns),
        out_specs=(rows, columns, columns, rows, columns),
        check_vma=False,
    )
```

time: 97.2 us -> 79.2 us (0.81)
  the two profiles are of different devices: /device:TPU:16 before, /device:TPU:1 now
where the time goes in v2:
time: 79.2 us; the launch traced here: 79 us
  Pallas kernels  78.4 us (99%)
    pallas_call x1, Pallas kernels, on_device(): pl.pallas_call(kernel, out_shape=(jax.ShapeDtypeStruct(stash.shape, BF16)...  76.1 us
    pallas_call x1, Pallas kernels, on_device(): pl.pallas_call(place, out_shape=tuple((jax.ShapeDtypeStruct(a.shape, a.dt...  2.25 us

profile of v2, /device:TPU:1, one launch (start us, length us, event | category | flops | bytes accessed | tf_op | source)
XLA Modules:
  0.0 79.0 jit_solution(13015402553921616447)
XLA Ops:
  0.6 76.1 %block_backward.1 = (bf16[10,768]{1,0:T(8,128)(2,1)}, bf16[768,256]{1,0:T(8,128)(2,1)}, bf16[768,256]{1,0:T(8,128)(2,1)}, bf16[256,768]{1,0:T(8,128)(2,1)}, bf16[288,768]{1,0:T(8,128)(2,1)}) custom-call(bf16[10,768]{1,0:T(8,128)(2,1)} %stash_in.1, bf16[10,768]{1,0:T(8,128)(2,1)} %mlp_in.1, bf16[80,288]{1,0:T(8,128)(2,1)} %qkv_in.1, bf16[768,256]{1,0:T(8,128)(2,1)} %wg_in.1, ...), custom_call_target="tpu_custom_call" | custom-call | flops 2600000000 | bytes 4000000 | tf_op jit(solution)/shard_map/block_backward/pallas_call | solution.py:416
  76.8 2.3 %place_results.1 = (bf16[10,768]{1,0:T(8,128)(2,1)}, bf16[768,256]{1,0:T(8,128)(2,1)}, bf16[768,256]{1,0:T(8,128)(2,1)}, bf16[256,768]{1,0:T(8,128)(2,1)}, bf16[288,768]{1,0:T(8,128)(2,1)}) custom-call(bf16[10,768]{1,0:T(8,128)(2,1)} %get-tuple-element.15.refs_0_, bf16[768,256]{1,0:T(8,128)(2,1)} %get-tuple-element.16.refs_1_, ...), custom_call_target="tpu_custom_call" | custom-call | tf_op jit(solution)/shard_map/place_results/pallas_call | solution.py:476

commit v3 on v2

--- a/solution.py
+++ b/solution.py
@@ -81,10 +81,11 @@
 
 def kernel(
     stash_in, mlp_in, qkv_in, wg_in, wu_in, wd_in, wq_in,
+    gi_hbm, gg_hbm, gu_hbm, gd_hbm, gq_hbm,
     gi_out, gg_out, gu_out, gd_out, gq_out,
     stash, mlp, qkv, wg, wu, wd, wq,
-    pad, packed, zin, shards, xs, xm, q, pf, sb, rb, cb, ab, hid, dg, du, gif, cr, rs1, rr1, own, z2, zr,
-    w_sem, z_ss, z_rs, g_ss, g_rs, x_ss, x_rs, q_ss, q_rs, s_ss, s_rs, a_ss, a_rs, c_ss, c_rs, r_ss, r_rs, e_ss, e_rs,
+    pad, packed, zin, shards, xs, xm, q, pf, sb, rb, cb, ab, hid, dg, du, gib, gif, cr, rs1, rr1, own, z2, zr,
+    w_sem, o_sem, z_ss, z_rs, g_ss, g_rs, x_ss, x_rs, q_ss, q_rs, s_ss, s_rs, a_ss, a_rs, c_ss, c_rs, r_ss, r_rs, e_ss, e_rs,
 ):
     y = lax.axis_index("gx")
     gy = lax.axis_index("gy")
@@ -107,6 +108,7 @@
     sibling = (y, hi * 2 + (1 - core), s)
 
     sends = []
+    stores = []
 
     def send(src, dst, ss, rs, device):
         copy = pltpu.make_async_remote_copy(
@@ -130,14 +132,14 @@
             )
         )
     ]
-    for copy in inputs:
-        copy.start()
     barrier = pltpu.get_barrier_semaphore()
     partners = [at_y(d) for d in (1, -1, 2, -2)] + [at_s(r) for r in range(1, NS)]
     partners += [at_hi(k) for k in range(1, NH)] + [sibling]
     for device in partners:
         pl.semaphore_signal(barrier, inc=1, device_id=device, device_id_type=MESH)
 
+    for copy in inputs:
+        copy.start()
     for copy in inputs[:3]:
         copy.wait()
     pad[...] = jnp.zeros_like(pad)
@@ -157,7 +159,7 @@
 
     shard_copies = {0: spread(0, packed)}
     z_copies = {
-        k: send(packed, zin.at[k], z_ss.at[k], z_rs.at[k], at_hi(-k)) for k in (2, 1, 3)
+        k: send(packed, zin.at[k], z_ss.at[k], z_rs.at[k], at_hi(-k)) for k in (1, 3, 2)
     }
 
     def wrap(d):
@@ -286,6 +288,12 @@
     def pass_results(k):
         pass_on(results[k], ab.at[k], a_ss.at[k], a_rs.at[k], LANES // 2)
 
+    def project_grad():
+        gq_out[...] = tn(flat(q), flat(xs)).astype(BF16)
+        early = pltpu.make_async_copy(gq_out, gq_hbm, o_sem.at[4])
+        early.start()
+        stores.append(early)
+
     halves = {}
 
     def input_partial(k):
@@ -307,15 +315,15 @@
             part += jnp.dot(q[block], wq[...], preferred_element_type=F32)
             return part
 
-        gif[k, 1] = partial(group(k) + 1 - core)
-        halves[k] = send(gif.at[k, 1], cr.at[k], c_ss.at[k], c_rs.at[k], sibling)
-        gif[k, 0] = partial(group(k) + core)
+        gib[k] = partial(group(k) + 1 - core).astype(BF16)
+        halves[k] = send(gib.at[k], cr.at[k], c_ss.at[k], c_rs.at[k], sibling)
+        gif[k] = partial(group(k) + core)
 
     pieces = {}
 
     def scatter_input(k):
         halves[k].wait_recv()
-        block = (gif[k, 0] + cr[k]).astype(BF16)
+        block = (gif[k] + cr[k].astype(F32)).astype(BF16)
         unpack = one_hot(NS * PAD, BLK, spreading)
         rs1[k] = (
             jnp.dot(unpack, block, preferred_element_type=F32).astype(BF16).reshape(NS, PAD, -1)
@@ -361,6 +369,7 @@
     gather_rows(3)
     project(3)
     input_partial(0)
+    project_grad()
     pass_results(1)
     elementwise(2)
     combine(3)
@@ -377,19 +386,29 @@
     input_partial(3)
     scatter_input(3)
     reduce_input(2)
+    def store(i, src, dst):
+        copy = pltpu.make_async_copy(src, dst, o_sem.at[i])
+        copy.start()
+        stores.append(copy)
+
     gg_out[...] = tn(flat(xs), flat(dg)).astype(BF16)
+    store(1, gg_out, gg_hbm)
     gu_out[...] = tn(flat(xs), flat(du)).astype(BF16)
+    store(2, gu_out, gu_hbm)
     reduce_input(3)
     gd_out[...] = tn(flat(hid), flat(xm)).astype(BF16)
-    gq_out[...] = tn(flat(q), flat(xs)).astype(BF16)
+    store(3, gd_out, gd_hbm)
     total = own[...]
     for copy in ends:
         copy.wait_recv()
     for k in range(1, NH):
         total = total + zr[k].astype(F32)
     gi_out[...] = total[0:ROWS].astype(BF16)
+    store(0, gi_out, gi_hbm)
     for copy in sends:
         copy.wait_send()
+    for copy in stores:
+        copy.wait()
 
 
 def place(*refs):
@@ -410,7 +429,6 @@
     width = stash.shape[1]
     units = w_gate.shape[1]
     proj = w_qkv.shape[1]
-    vmem = pl.BlockSpec(memory_space=pltpu.VMEM)
     hbm = pl.BlockSpec(memory_space=pltpu.HBM)
     dma = pltpu.SemaphoreType.DMA
     results = pl.pallas_call(
@@ -423,8 +441,13 @@
             jax.ShapeDtypeStruct((proj, width), BF16),
         ),
         in_specs=[hbm] * 7,
-        out_specs=(vmem,) * 5,
+        out_specs=(hbm,) * 5,
         scratch_shapes=[
+            pltpu.VMEM(stash.shape, BF16),
+            pltpu.VMEM(w_gate.shape, BF16),
+            pltpu.VMEM(w_up.shape, BF16),
+            pltpu.VMEM(w_down.shape, BF16),
+            pltpu.VMEM((proj, width), BF16),
             pltpu.VMEM(stash.shape, BF16),
             pltpu.VMEM(mlp_grad.shape, BF16),
             pltpu.VMEM(qkv_grad.shape, BF16),
@@ -447,8 +470,9 @@
             pltpu.VMEM((NY, BLK, units), BF16),
             pltpu.VMEM((NY, BLK, units), BF16),
             pltpu.VMEM((NY, BLK, units), BF16),
-            pltpu.VMEM((NH, 2, BLK, width), F32),
+            pltpu.VMEM((NH, BLK, width), BF16),
             pltpu.VMEM((NH, BLK, width), F32),
+            pltpu.VMEM((NH, BLK, width), BF16),
             pltpu.VMEM((NH, NS, PAD, width), BF16),
             pltpu.VMEM((NH, NS, PAD, width), BF16),
             pltpu.VMEM((PAD, width), F32),
@@ -456,6 +480,7 @@
             pltpu.VMEM((NH, PAD, width), BF16),
         ]
         + [dma((7,))]
+        + [dma((5,))]
         + [dma((NH,))] * 2
         + [dma((NH, NS))] * 2
         + [dma((NH, 2))] * 2

time: 79.2 us -> 76.3 us (0.963)
  Pallas kernels: 78.4 us -> 75.5 us
    pallas_call x1, Pallas kernels: 76.1 us -> 73.2 us  [on_device(): pl.pallas_call(kernel, out_shape=(jax.ShapeDtypeStruct(stash.shape, BF16)...]
where the time goes in v3:
time: 76.3 us; the launch traced here: 76.1 us
  Pallas kernels  75.5 us (99%)
    pallas_call x1, Pallas kernels, on_device(): pl.pallas_call(kernel, out_shape=(jax.ShapeDtypeStruct(stash.shape, BF16)...  73.2 us
    pallas_call x1, Pallas kernels, on_device(): pl.pallas_call(place, out_shape=tuple((jax.ShapeDtypeStruct(a.shape, a.dt...  2.25 us

profile of v3, /device:TPU:1, one launch (start us, length us, event | category | flops | bytes accessed | tf_op | source)
XLA Modules:
  0.0 76.1 jit_solution(18191509727967566916)
XLA Ops:
  0.6 73.2 %block_backward.1 = (bf16[10,768]{1,0:T(8,128)(2,1)}, bf16[768,256]{1,0:T(8,128)(2,1)}, bf16[768,256]{1,0:T(8,128)(2,1)}, bf16[256,768]{1,0:T(8,128)(2,1)}, bf16[288,768]{1,0:T(8,128)(2,1)}) custom-call(bf16[10,768]{1,0:T(8,128)(2,1)} %stash_in.1, bf16[10,768]{1,0:T(8,128)(2,1)} %mlp_in.1, bf16[80,288]{1,0:T(8,128)(2,1)} %qkv_in.1, bf16[768,256]{1,0:T(8,128)(2,1)} %wg_in.1, ...), custom_call_target="tpu_custom_call" | custom-call | flops 2600000000 | bytes 4000000 | tf_op jit(solution)/shard_map/block_backward/pallas_call | solution.py:434
  73.9 2.3 %place_results.1 = (bf16[10,768]{1,0:T(8,128)(2,1)}, bf16[768,256]{1,0:T(8,128)(2,1)}, bf16[768,256]{1,0:T(8,128)(2,1)}, bf16[256,768]{1,0:T(8,128)(2,1)}, bf16[288,768]{1,0:T(8,128)(2,1)}) custom-call(bf16[10,768]{1,0:T(8,128)(2,1)} %get-tuple-element.15.refs_0_, bf16[768,256]{1,0:T(8,128)(2,1)} %get-tuple-element.16.refs_1_, ...), custom_call_target="tpu_custom_call" | custom-call | tf_op jit(solution)/shard_map/place_results/pallas_call | solution.py:501

commit v4 on v3

--- a/solution.py
+++ b/solution.py
@@ -159,7 +159,7 @@
 
     shard_copies = {0: spread(0, packed)}
     z_copies = {
-        k: send(packed, zin.at[k], z_ss.at[k], z_rs.at[k], at_hi(-k)) for k in (1, 3, 2)
+        k: send(packed, zin.at[k], z_ss.at[k], z_rs.at[k], at_hi(-k)) for k in (1, 2, 3)
     }
 
     def wrap(d):
@@ -414,8 +414,14 @@
 def place(*refs):
     ins, outs, held = refs[:5], refs[5:10], refs[10:15]
     in_sems, out_sems = refs[15:]
-    loads = [pltpu.make_async_copy(ins[i], held[i], in_sems.at[i]) for i in range(5)]
-    stores = [pltpu.make_async_copy(held[i], outs[i], out_sems.at[i]) for i in range(5)]
+    loads, stores = [], []
+    for i in range(5):
+        rows = ins[i].shape[0]
+        cuts = (0, rows) if rows < 2 * PAD else (0, rows // 2, rows)
+        for h in range(len(cuts) - 1):
+            part = pl.ds(cuts[h], cuts[h + 1] - cuts[h])
+            loads.append(pltpu.make_async_copy(ins[i].at[part], held[i].at[part], in_sems.at[i, h]))
+            stores.append(pltpu.make_async_copy(held[i].at[part], outs[i].at[part], out_sems.at[i, h]))
     for copy in loads:
         copy.start()
     for load, store in zip(loads, stores):
@@ -503,7 +509,7 @@
         out_shape=tuple(jax.ShapeDtypeStruct(a.shape, a.dtype) for a in results),
         in_specs=[hbm] * 5,
         out_specs=(hbm,) * 5,
-        scratch_shapes=[pltpu.VMEM(a.shape, a.dtype) for a in results] + [dma((5,))] * 2,
+        scratch_shapes=[pltpu.VMEM(a.shape, a.dtype) for a in results] + [dma((5, 2))] * 2,
         compiler_params=pltpu.CompilerParams(vmem_limit_bytes=63 * 2**20),
         name="place_results",
     )(*results)

time: 76.3 us -> 76.1 us (level)
  no operation moved by 1% of the time
where the time goes in v4:
time: 76.1 us; the launch traced here: 76 us
  Pallas kernels  75.3 us (99%)
    pallas_call x1, Pallas kernels, on_device(): pl.pallas_call(kernel, out_shape=(jax.ShapeDtypeStruct(stash.shape, BF16)...  73 us
    pallas_call x1, Pallas kernels, on_device(): pl.pallas_call(place, out_shape=tuple((jax.ShapeDtypeStruct(a.shape, a.dt...  2.36 us

profile of v4, /device:TPU:1, one launch (start us, length us, event | category | flops | bytes accessed | tf_op | source)
XLA Modules:
  0.0 76.0 jit_solution(15312554213778551508)
XLA Ops:
  0.6 73.0 %block_backward.1 = (bf16[10,768]{1,0:T(8,128)(2,1)}, bf16[768,256]{1,0:T(8,128)(2,1)}, bf16[768,256]{1,0:T(8,128)(2,1)}, bf16[256,768]{1,0:T(8,128)(2,1)}, bf16[288,768]{1,0:T(8,128)(2,1)}) custom-call(bf16[10,768]{1,0:T(8,128)(2,1)} %stash_in.1, bf16[10,768]{1,0:T(8,128)(2,1)} %mlp_in.1, bf16[80,288]{1,0:T(8,128)(2,1)} %qkv_in.1, bf16[768,256]{1,0:T(8,128)(2,1)} %wg_in.1, ...), custom_call_target="tpu_custom_call" | custom-call | flops 2600000000 | bytes 4000000 | tf_op jit(solution)/shard_map/block_backward/pallas_call | solution.py:440
  73.6 2.4 %place_results.1 = (bf16[10,768]{1,0:T(8,128)(2,1)}, bf16[768,256]{1,0:T(8,128)(2,1)}, bf16[768,256]{1,0:T(8,128)(2,1)}, bf16[256,768]{1,0:T(8,128)(2,1)}, bf16[288,768]{1,0:T(8,128)(2,1)}) custom-call(bf16[10,768]{1,0:T(8,128)(2,1)} %get-tuple-element.15.refs_0_, bf16[768,256]{1,0:T(8,128)(2,1)} %get-tuple-element.16.refs_1_, ...), custom_call_target="tpu_custom_call" | custom-call | tf_op jit(solution)/shard_map/place_results/pallas_call | solution.py:507
